TPU v7x, 32 devices: a whole 2x2x4 slice. The times are simulated.
32 devices in a mesh: gx: 4 (over z), gy: 8 (over y, x, core).
Axes of the slice: x: 2, y: 2, z: 4, core: 2. Of those that a mesh axis runs over, the one named last changes fastest.
Arguments:
- control: float32 [4, 64, 64, 2048], P(None, None, 'gx', 'gy'), may hold values from -6 to 6
- background: float32 [4, 64, 64, 2048], P(None, None, 'gx', 'gy'), may hold values from -6 to 6
- vert_factor: float32 [4, 64, 64], replicated, may hold values from -0.75 to 0.75
- length_rates: float32 [2, 4, 64], replicated, may hold values from 0.5 to 40
- flash_weights: float32 [4, 64], replicated, may hold values from -3 to 3
- level_weights: float32 [64], replicated, may hold values from -0.75 to 0.75
- obs_owner: int32 [16384, 1], P(('gx', 'gy')), may hold values from 0 to 31; in each aligned block of 512 rows (0 to 511, 512 to 1023, ...) at most 32 rows name the same one
- obs_cell: int32 [16384], P(('gx', 'gy')), may hold values from 0 to 4095
- obs_count: int32 [32], P(('gx', 'gy')), may hold values from 256 to 512, as said below
- flash_obs: float32 [16384], P(('gx', 'gy')), may hold values from 0.1 to 3
- obs_error: float32 [16384], P(('gx', 'gy')), may hold values from 0.3 to 1
Outputs:
- grad: float32 [4, 64, 64, 2048], P(None, None, 'gx', 'gy')
- departure: float32 [16384], P(('gx', 'gy'))
Inputs may be any that keep to these rules, and one draw needn't show every extreme that they name: `obs_owner`: among one device's 512 slots no owner is named more than 32 times, a bound that some block reaches. Only the first obs_count slots of a device are live; some device has all 512 live.
All inputs are finite; a program needn't handle non-finite values.
Results may differ from a plain program's by a relative error of at most 0.0003.
Values sent between devices are 32-bit elements; how exact they have to be, the bound alone decides.
A program may use at most 128 MiB of HBM per device.

v0:
```python
import functools
import jax
import jax.numpy as jnp
from jax import lax
from jax.experimental import pallas as pl
from jax.experimental.pallas import tpu as pltpu
from jax.sharding import PartitionSpec as P

LANES = 128
MESH = pl.DeviceIdType.MESH
f32, bf16 = jnp.float32, jnp.bfloat16


def split(value):
    high = value.astype(bf16)
    return high, (value - high.astype(f32)).astype(bf16)


def dot(left, right):
    return jnp.dot(left, right, preferred_element_type=f32)


def kernel(
    nx, ny, variables, levels, rx, ry,
    ctrl, bg, tab, lwt, forward, backward, obs, seen,
    out, dep,
    field, sums, sp_all, obs_all, edge, edge_b, q_ref, xin, xout, xin_b, xout_b, row0, axt, stage, base_levels, mstack, bstack,
    obs_s, obs_r, sp_s, sp_r, e_s, e_r, f_s, f_r, x_s, x_r, b_s, b_r,
):
    devices = nx * ny
    gx, gy = lax.axis_index("gx"), lax.axis_index("gy")
    me = gx * ny + gy
    halves = ry // LANES
    tiles = levels // 8
    vk = variables * levels
    lane = lax.broadcasted_iota(jnp.int32, (8, LANES), 1)
    lane_f = lane.astype(f32)
    shifts = [1 << s for s in range(7)]

    def peer(offset):
        other = lax.rem(me + offset, devices)
        return (other // ny, lax.rem(other, ny))

    def to_all(ref, send, recv):
        def one(offset):
            return pltpu.make_async_remote_copy(
                ref.at[me], ref.at[me], send.at[offset], recv.at[me], peer(offset), MESH
            )
        return one

    def from_all(ref, send, recv, offset):
        src = lax.rem(me + offset, devices)
        return pltpu.make_async_remote_copy(
            ref.at[src], ref.at[src], send.at[offset], recv.at[src], peer(offset), MESH
        )

    def start_all(ref, send, recv):
        @pl.loop(1, devices)
        def _(offset):
            to_all(ref, send, recv)(offset).start()

    def wait_all(ref, send, recv):
        @pl.loop(1, devices)
        def _(offset):
            from_all(ref, send, recv, offset).wait_recv()
            to_all(ref, send, recv)(offset).wait_send()

    def row_copy(ref, send, recv, offset, slot):
        other = lax.rem(gy + offset, ny)
        return pltpu.make_async_remote_copy(
            ref.at[slot], ref.at[slot], send.at[offset], recv.at[slot], (gx, other), MESH
        )

    def start_row(ref, send, recv):
        @pl.loop(1, ny)
        def _(offset):
            row_copy(ref, send, recv, offset, gy).start()

    def wait_row(ref, send, recv):
        @pl.loop(1, ny)
        def _(offset):
            row_copy(ref, send, recv, offset, lax.rem(gy + offset, ny)).wait_recv()
            row_copy(ref, send, recv, offset, gy).wait_send()

    def chain(v, source, target, send, recv, other):
        return pltpu.make_async_remote_copy(
            source.at[v], target.at[v], send.at[v], recv.at[v], (other, gy), MESH
        )

    def half(h):
        return slice(h * LANES, (h + 1) * LANES)

    def rates(v, tile):
        rows = pl.ds(tile * 8, 8)
        return tab[v, rows, :], tab[variables + v, rows, :]

    def scan_y(parts, coefs, reach, reverse):
        done = [None] * halves
        carry = None
        for h in (range(halves)[::-1] if reverse else range(halves)):
            part = parts[h]
            for s, c in zip(shifts, coefs):
                part = part + c * pltpu.roll(part, LANES - s if reverse else s, 1)
            if carry is not None:
                part = part + reach * carry
            end = part[:, :1] if reverse else part[:, LANES - 1:]
            carry = jnp.broadcast_to(end, part.shape)
            done[h] = part
        return done, carry

    def forward_coefs(sy):
        return [jnp.where(lane >= s, jnp.exp(-sy * s), 0.0) for s in shifts]

    def backward_coefs(sy):
        return [jnp.where(lane < LANES - s, jnp.exp(-sy * s), 0.0) for s in shifts]

    barrier = pltpu.get_barrier_semaphore()

    @pl.loop(1, devices)
    def _(offset):
        pl.semaphore_signal(barrier, inc=1, device_id=peer(offset), device_id_type=MESH)
    pl.semaphore_wait(barrier, devices - 1)

    obs_all[me] = obs[...]
    start_all(obs_all, obs_s, obs_r)

    high, low = split(forward[...])
    mstack[...] = jnp.concatenate([high, low], axis=0)
    high, low = split(backward[...])
    bstack[...] = jnp.concatenate([high, high, low], axis=1)

    edge[gy] = jnp.zeros((levels, LANES), f32)
    edge_b[gy] = jnp.zeros((levels, LANES), f32)

    @pl.loop(0, variables * tiles)
    def _(i):
        v, tile = i // tiles, lax.rem(i, tiles)
        sx, sy = rates(v, tile)
        coefs = forward_coefs(sy)
        reach = jnp.exp(-sy * (lane_f + 1.0))
        ax = jnp.exp(-sx)
        axt[pl.ds(i * 8, 8), :] = ax
        for h in range(halves):
            stage[h] = ctrl[v, pl.ds(tile * 8 * rx, 8 * rx), half(h)]
        state = [jnp.zeros((8, LANES), f32)] * halves
        column = edge[gy, pl.ds(tile * 8, 8), :]
        for x in range(rx):
            parts = [stage[h, pl.ds(x, 8, stride=rx), :] for h in range(halves)]
            parts, last = scan_y(parts, coefs, reach, False)
            column = jnp.where(lane == v * rx + x, last, column)
            for h in range(halves):
                state[h] = ax * state[h] + parts[h]
                field[x, pl.ds(i * 8, 8), half(h)] = state[h]
        edge[gy, pl.ds(tile * 8, 8), :] = column

    start_row(edge, e_s, e_r)

    @pl.loop(0, tiles)
    def _(tile):
        for v in range(variables):
            for h in range(halves):
                stage[v * halves + h] = bg[v, pl.ds(tile * 8 * rx, 8 * rx), half(h)]
        weights = [tab[2 * variables + v, pl.ds(tile * 8, 8), :] for v in range(variables)]
        for x in range(rx):
            for h in range(halves):
                part = jnp.zeros((8, LANES), f32)
                for v in range(variables):
                    part = part + weights[v] * stage[v * halves + h, pl.ds(x, 8, stride=rx), :]
                base_levels[x, pl.ds(tile * 8, 8), half(h)] = part

    wait_all(obs_all, obs_s, obs_r)
    sums[...] = jnp.zeros_like(sums)
    per = obs.shape[1]
    row_x = lax.broadcasted_iota(jnp.int32, (rx, per), 0).astype(f32)
    row_y = lax.broadcasted_iota(jnp.int32, (ry, per), 0).astype(f32)
    base = (me * rx).astype(f32)

    @pl.loop(0, devices)
    def _(src):
        total = sums[...]
        for part in range(2):
            key = obs_all[src, part:part + 1, :] - base
            spot = obs_all[src, 2 + part:3 + part, :]
            hit = row_x == key
            pieces = []
            for field_of in (4, 6):
                weight = obs_all[src, field_of + part:field_of + part + 1, :]
                pieces += split(jnp.where(hit, weight, 0.0))
            left = jnp.concatenate(pieces, axis=0)
            right = jnp.where(row_y == spot, 1.0, 0.0).astype(bf16)
            total = total + lax.dot_general(
                left, right, (((1,), (1,)), ((), ())), preferred_element_type=f32
            )
        sums[...] = total

    @pl.when(gx == 0)
    def _():
        xin[...] = jnp.zeros_like(xin)

    @pl.when(gx == nx - 1)
    def _():
        xin_b[...] = jnp.zeros_like(xin_b)

    def rates_in_lanes(tile):
        wide = [jnp.zeros((8, LANES), f32)] * 2
        for v in range(variables):
            here = (lane >= v * rx) & (lane < (v + 1) * rx)
            wide = [jnp.where(here, new, old) for new, old in zip(rates(v, tile), wide)]
        return wide

    wait_row(edge, e_s, e_r)

    @pl.loop(0, tiles)
    def _(tile):
        rows = pl.ds(tile * 8, 8)
        sx, sy = rates_in_lanes(tile)
        total = jnp.zeros((8, LANES), f32)
        for src in range(ny):
            far = jnp.maximum(gy - 1 - src, 0).astype(f32) * ry
            total = total + jnp.where(src < gy, jnp.exp(-sy * far) * edge[src, rows, :], 0.0)
        inner = lax.rem(lane, rx)
        s = 1
        while s < rx:
            total = total + jnp.where(inner >= s, jnp.exp(-sx * s), 0.0) * pltpu.roll(total, s, 1)
            s *= 2
        q_ref[rows, :] = total

    for v in range(variables):
        @pl.when(gx > 0)
        def _():
            chain(v, xout, xin, x_s, x_r, gx).wait_recv()

        @pl.when(gx < nx - 1)
        def _():
            @pl.loop(0, tiles)
            def _(tile):
                rows = pl.ds(tile * 8, 8)
                sx, sy = rates(v, tile)
                spot = v * rx + rx - 1
                q = jnp.broadcast_to(q_ref[rows, spot:spot + 1], (8, LANES))
                for h in range(halves):
                    xout[v, rows, half(h)] = (
                        field[rx - 1, pl.ds(v * levels + tile * 8, 8), half(h)]
                        + jnp.exp(-sy * (lane_f + (1.0 + h * LANES))) * q
                        + jnp.exp(-sx * rx) * xin[v, rows, half(h)]
                    )
            chain(v, xout, xin, x_s, x_r, gx + 1).start()

        @pl.loop(0, tiles)
        def _(tile):
            rows = pl.ds(tile * 8, 8)
            sx, sy = rates(v, tile)
            reach = [jnp.exp(-sy * (lane_f + (1.0 + h * LANES))) for h in range(halves)]
            q_all = q_ref[rows, :]
            ax = jnp.exp(-sx)
            entering = [xin[v, rows, half(h)] for h in range(halves)]
            for x in range(rx):
                q = jnp.broadcast_to(q_all[:, v * rx + x:v * rx + x + 1], (8, LANES))
                for h in range(halves):
                    entering[h] = ax * entering[h]
                    at = (x, pl.ds(v * levels + tile * 8, 8), half(h))
                    field[at] = field[at] + reach[h] * q + entering[h]

    row0[...] = jnp.zeros_like(row0)
    wide = lambda value: jnp.concatenate([value] * halves, axis=1)

    @pl.loop(0, rx)
    def _(i):
        x = rx - 1 - i
        high, low = split(field[x])
        both = dot(mstack[...], high)
        value = both[:levels] + both[levels:] + dot(mstack[:levels, :], low)
        value = value + base_levels[x]
        small = jnp.exp(-jnp.abs(value))
        soft = jnp.maximum(value, 0.0) + jnp.log1p(small)
        slope = jnp.where(value >= 0, 1.0, small) / (1.0 + small)
        total = jnp.sum(wide(lwt[...]) * soft, axis=0, keepdims=True)
        small = jnp.exp(-jnp.abs(total))
        sp = jnp.maximum(total, 0.0) + jnp.log1p(small)
        sg = jnp.where(total >= 0, 1.0, small) / (1.0 + small)
        sp_all[me, pl.ds(x, 1), :] = sp
        s1 = sums[pl.ds(x, 1), :] + sums[pl.ds(rx + x, 1), :]
        s2 = sums[pl.ds(2 * rx + x, 1), :] + sums[pl.ds(3 * rx + x, 1), :]
        high, low = split(sg * (sp * s1 - s2) * slope)
        back = dot(bstack[...], jnp.concatenate([high, low, high], axis=0))
        now = wide(axt[...]) * row0[...] + back
        row0[...] = now
        field[x] = now

    start_all(sp_all, sp_s, sp_r)

    for v in range(variables):
        @pl.loop(0, tiles)
        def _(tile):
            sx, sy = rates(v, tile)
            coefs = backward_coefs(sy)
            reach = jnp.exp(-sy * (LANES - lane_f))
            for x in range(rx):
                rows = pl.ds(v * levels + tile * 8, 8)
                parts = [field[x, rows, half(h)] for h in range(halves)]
                parts, _ = scan_y(parts, coefs, reach, True)
                for h in range(halves):
                    field[x, rows, half(h)] = parts[h]

        @pl.when(gx < nx - 1)
        def _():
            chain(v, xout_b, xin_b, b_s, b_r, gx).wait_recv()

        @pl.when(gx > 0)
        def _():
            xout_b[v] = row0[v * levels:(v + 1) * levels, :] + wide(
                jnp.exp(-tab[v] * rx)
            ) * xin_b[v]
            chain(v, xout_b, xin_b, b_s, b_r, gx - 1).start()

        @pl.loop(0, tiles)
        def _(tile):
            rows = pl.ds(tile * 8, 8)
            sx, sy = rates(v, tile)
            parts = [xin_b[v, rows, half(h)] for h in range(halves)]
            parts, first = scan_y(
                parts, backward_coefs(sy), jnp.exp(-sy * (LANES - lane_f)), True
            )
            for h in range(halves):
                row0[pl.ds(v * levels + tile * 8, 8), half(h)] = parts[h]
            column = edge_b[gy, rows, :]
            for x in range(rx):
                own = field[x, pl.ds(v * levels + tile * 8, 8), :LANES][:, :1]
                whole = jnp.broadcast_to(own, (8, LANES)) + jnp.exp(-sx * (rx - x)) * first
                column = jnp.where(lane == v * rx + x, whole, column)
            edge_b[gy, rows, :] = column

    start_row(edge_b, f_s, f_r)

    wait_all(sp_all, sp_s, sp_r)
    count = seen.shape[1]
    key, flash = seen[0:1, :], seen[2:3, :]
    column_y = lax.broadcasted_iota(jnp.int32, (ry, count), 0).astype(f32)
    pick = jnp.where(column_y == seen[1:2, :], 1.0, 0.0).astype(bf16)
    row_of = lax.broadcasted_iota(jnp.int32, (rx, count), 0).astype(f32)

    def find(src, found):
        high, low = split(sp_all[src])
        value = dot(jnp.concatenate([high, low], axis=0), pick)
        value = value[:rx] + value[rx:]
        return found + jnp.where(row_of == key - (src * rx).astype(f32), value, 0.0)

    found = lax.fori_loop(0, devices, find, jnp.zeros((rx, count), f32))
    found = jnp.sum(found, axis=0, keepdims=True)
    dep[...] = jnp.where(key >= 0, found - flash, 0.0)

    wait_row(edge_b, f_s, f_r)

    @pl.loop(0, tiles)
    def _(tile):
        rows = pl.ds(tile * 8, 8)
        sx, sy = rates_in_lanes(tile)
        total = jnp.zeros((8, LANES), f32)
        for src in range(ny):
            far = jnp.maximum(src - gy - 1, 0).astype(f32) * ry
            total = total + jnp.where(src > gy, jnp.exp(-sy * far) * edge_b[src, rows, :], 0.0)
        for v in range(variables):
            sx, sy = rates(v, tile)
            reach = [jnp.exp(-sy * (ry - h * LANES - lane_f)) for h in range(halves)]
            ax = jnp.exp(-sx)
            mine = pl.ds(v * levels + tile * 8, 8)
            entering = [row0[mine, half(h)] for h in range(halves)]
            for x in range(rx)[::-1]:
                q = jnp.broadcast_to(total[:, v * rx + x:v * rx + x + 1], (8, LANES))
                for h in range(halves):
                    entering[h] = ax * entering[h]
                    stage[v * halves + h, pl.ds(x, 8, stride=rx), :] = (
                        field[x, mine, half(h)] + reach[h] * q + entering[h]
                    )
            for h in range(halves):
                at = (v, pl.ds(tile * 8 * rx, 8 * rx), half(h))
                out[at] = ctrl[at] + stage[v * halves + h]

    for v in range(variables):
        @pl.when(gx < nx - 1)
        def _():
            chain(v, xout, xin, x_s, x_r, gx + 1).wait_send()

        @pl.when(gx > 0)
        def _():
            chain(v, xout_b, xin_b, b_s, b_r, gx - 1).wait_send()


def body(
    control, background, vert_factor, length_rates, flash_weights, level_weights,
    obs_owner, obs_cell, obs_count, flash_obs, obs_error,
):
    variables, levels, rx, ry = control.shape
    nx, ny = lax.axis_size("gx"), lax.axis_size("gy")
    devices = nx * ny
    count = obs_cell.shape[0]
    vk = variables * levels
    step_x = length_rates[0] / (rx * nx)
    step_y = length_rates[1] / (ry * ny)
    gain = jnp.sqrt(jnp.expm1(-2.0 * step_x) * jnp.expm1(-2.0 * step_y))
    forward = flash_weights[:, :, None] * vert_factor * gain[:, None, :]
    forward = forward.transpose(1, 0, 2).reshape(levels, vk)
    backward = (flash_weights * level_weights)[:, :, None] * vert_factor * gain[:, None, :]
    backward = backward.transpose(0, 2, 1).reshape(vk, levels)
    tab = jnp.concatenate([step_x, step_y, flash_weights], axis=0)
    tab = jnp.broadcast_to(tab[:, :, None], (3 * variables, levels, LANES))
    lwt = jnp.broadcast_to(level_weights[:, None], (levels, LANES))

    live = jnp.arange(count) < obs_count[0]
    key = jnp.where(live, obs_owner[:, 0] * rx + obs_cell // ry, -1).astype(f32)
    spot = (obs_cell % ry).astype(f32)
    weight = 1.0 / (obs_error * obs_error)
    obs = jnp.stack([key, spot, weight, flash_obs * weight]).reshape(8, count // 2)
    zero = jnp.zeros_like(key)
    seen = jnp.stack([key, spot, flash_obs, zero, zero, zero, zero, zero])

    vmem = pl.BlockSpec(memory_space=pltpu.VMEM)
    dma = pltpu.SemaphoreType.DMA
    grad, departure = pl.pallas_call(
        functools.partial(kernel, nx, ny, variables, levels, rx, ry),
        out_shape=(
            jax.ShapeDtypeStruct((variables, levels * rx, ry), f32),
            jax.ShapeDtypeStruct((1, count), f32),
        ),
        in_specs=[vmem] * 8,
        out_specs=(vmem, vmem),
        scratch_shapes=[
            pltpu.VMEM((rx, vk, ry), f32),
            pltpu.VMEM((4 * rx, ry), f32),
            pltpu.VMEM((devices, rx, ry), f32),
            pltpu.VMEM((devices, 8, count // 2), f32),
            pltpu.VMEM((ny, levels, LANES), f32),
            pltpu.VMEM((ny, levels, LANES), f32),
            pltpu.VMEM((levels, LANES), f32),
            pltpu.VMEM((variables, levels, ry), f32),
            pltpu.VMEM((variables, levels, ry), f32),
            pltpu.VMEM((variables, levels, ry), f32),
            pltpu.VMEM((variables, levels, ry), f32),
            pltpu.VMEM((vk, ry), f32),
            pltpu.VMEM((vk, LANES), f32),
            pltpu.VMEM((variables * ry // LANES, 8 * rx, LANES), f32),
            pltpu.VMEM((rx, levels, ry), f32),
            pltpu.VMEM((2 * levels, vk), bf16),
            pltpu.VMEM((vk, 3 * levels), bf16),
            dma((devices,)), dma((devices,)), dma((devices,)), dma((devices,)),
            dma((ny,)), dma((ny,)), dma((ny,)), dma((ny,)),
            dma((variables,)), dma((variables,)), dma((variables,)), dma((variables,)),
        ],
        compiler_params=pltpu.CompilerParams(
            collective_id=0, has_side_effects=True, vmem_limit_bytes=48 * 2**20
        ),
    )(
        control.reshape(variables, levels * rx, ry),
        background.reshape(variables, levels * rx, ry),
        tab, lwt, forward, backward, obs, seen,
    )
    return grad.reshape(control.shape), departure.reshape(count)


def solution(mesh):
    placed = (
        P(None, None, "gx", "gy"),
        P(None, None, "gx", "gy"),
        P(),
        P(),
        P(),
        P(),
        P(("gx", "gy"), None),
        P(("gx", "gy")),
        P(("gx", "gy")),
        P(("gx", "gy")),
        P(("gx", "gy")),
    )
    return jax.shard_map(
        body,
        mesh=mesh,
        in_specs=placed,
        out_specs=(P(None, None, "gx", "gy"), P(("gx", "gy"))),
        check_vma=False,
    )
```

profile of v0, /device:TPU:0, one launch (start us, length us, event | category | flops | bytes accessed | tf_op | source)
XLA Modules:
  0.0 142.1 jit_solution(13161972357709186910)
XLA Ops:
  1.3 0.7 broadcast_multiply_fusion
  2.0 0.7 fusion.2
  2.7 0.7 broadcast_multiply_fusion.1
  3.3 0.7 multiply_divide_fusion
  4.1 0.7 sqrt_bitcast_fusion
  4.8 0.7 pad_maximum_fusion
  5.5 0.7 stack.33.seen
  6.2 0.7 broadcast_in_dim.6.lwt
  6.9 1.0 multiply_bitcast_fusion
  8.0 0.1 copy.14
  8.1 0.1 copy.13
  8.2 0.1 reshape.60.forward
  8.3 0.2 broadcast_in_dim.5.tab
  8.5 131.0 %shard_map.122 = (f32[4,1024,256]{2,1,0:T(8,128)S(1)}, f32[1,512]{1,0:T(1,128)S(1)}) custom-call(f32[4,1024,256]{2,1,0:T(8,128)} %bitcast.26, f32[4,1024,256]{2,1,0:T(8,128)} %bitcast.27, f32[12,64,128]{2,1,0:T(8,128)S(1)} %broadcast_in_dim.5.tab, f32[64,128]{1,0:T(8,128)S(1)} %broadcast_in_dim.6.lwt, f32[64,256]{1,0:T(8,128)S(1)} %reshape.60.forward, ...), custom_call_target="tpu_custom_call" | custom-call | tf_op jit(solution)/shard_map/pallas_call | solution.py:419
  139.5 2.0 %copy.18 = f32[4,64,16,256]{3,2,1,0:T(8,128)} copy(f32[4,64,16,256]{3,2,1,0:T(8,128)S(1)} %bitcast.23) | data formatting | bytes 8388608
  141.5 0.6 copy.19
  (4 shorter events, 0.0 us)
where the time goes:
time: 142 us
  Pallas kernels  131 us (92%)
  other arithmetic  5.24 us (4%)
  local copies, waits for them, and re-layouts  4.52 us (3%)
    pallas_call x1, Pallas kernels, body(): pl.pallas_call(functools.partial(kernel, nx, ny, variables, levels, rx, r...  131 us

commit v1 on v0

v1 whole, which is shorter than its diff:
```python
import functools
import jax
import jax.numpy as jnp
from jax import lax
from jax.experimental import pallas as pl
from jax.experimental.pallas import tpu as pltpu
from jax.sharding import PartitionSpec as P

LANES = 128
MESH = pl.DeviceIdType.MESH
f32, bf16 = jnp.float32, jnp.bfloat16


def split(value):
    high = value.astype(bf16)
    return high, (value - high.astype(f32)).astype(bf16)


def dot(left, right):
    return jnp.dot(left, right, preferred_element_type=f32)


def kernel(
    nx, ny, variables, levels, rx, ry,
    ctrl, bg, vert, rate, gain, flash_w, level_w, seen,
    out, dep,
    field, sums, sp_all, obs_all, edge, edge_b, q_ref, xin, xout, xin_b, xout_b, row0, axt, stage,
    base_levels, mstack, bstack, tab, raw, tri, tri_b, grow, fade, slopes, totals,
    obs_s, obs_r, sp_s, sp_r, e_s, e_r, f_s, f_r, x_s, x_r, b_s, b_r,
):
    devices = nx * ny
    gx, gy = lax.axis_index("gx"), lax.axis_index("gy")
    me = gx * ny + gy
    halves = ry // LANES
    tiles = levels // 8
    vk = variables * levels
    lane = lax.broadcasted_iota(jnp.int32, (8, LANES), 1)
    def peer(offset):
        other = lax.rem(me + offset, devices)
        return (other // ny, lax.rem(other, ny))

    def to_all(ref, send, recv):
        def one(offset):
            return pltpu.make_async_remote_copy(
                ref.at[me], ref.at[me], send.at[offset], recv.at[me], peer(offset), MESH
            )
        return one

    def from_all(ref, send, recv, offset):
        src = lax.rem(me + offset, devices)
        return pltpu.make_async_remote_copy(
            ref.at[src], ref.at[src], send.at[offset], recv.at[src], peer(offset), MESH
        )

    def start_all(ref, send, recv):
        @pl.loop(1, devices)
        def _(offset):
            to_all(ref, send, recv)(offset).start()

    def wait_all(ref, send, recv):
        @pl.loop(1, devices)
        def _(offset):
            from_all(ref, send, recv, offset).wait_recv()
            to_all(ref, send, recv)(offset).wait_send()

    def row_copy(ref, send, recv, offset, slot):
        other = lax.rem(gy + offset, ny)
        return pltpu.make_async_remote_copy(
            ref.at[slot], ref.at[slot], send.at[offset], recv.at[slot], (gx, other), MESH
        )

    def start_row(ref, send, recv):
        @pl.loop(1, ny)
        def _(offset):
            row_copy(ref, send, recv, offset, gy).start()

    def wait_row(ref, send, recv):
        @pl.loop(1, ny)
        def _(offset):
            row_copy(ref, send, recv, offset, lax.rem(gy + offset, ny)).wait_recv()
            row_copy(ref, send, recv, offset, gy).wait_send()

    def chain(v, source, target, send, recv, other):
        return pltpu.make_async_remote_copy(
            source.at[v], target.at[v], send.at[v], recv.at[v], (other, gy), MESH
        )

    def half(h):
        return slice(h * LANES, (h + 1) * LANES)

    def rates(v, tile):
        rows = pl.ds(tile * 8, 8)
        return tab[v, rows, :], tab[variables + v, rows, :]

    barrier = pltpu.get_barrier_semaphore()

    @pl.loop(1, devices)
    def _(offset):
        pl.semaphore_signal(barrier, inc=1, device_id=peer(offset), device_id_type=MESH)
    pl.semaphore_wait(barrier, devices - 1)

    count = seen.shape[1]
    per = count // 2
    cell_x = jnp.floor(seen[1:2, :] * (1.0 / ry))
    cell_y = seen[1:2, :] - cell_x * ry
    place = lax.broadcasted_iota(jnp.int32, (1, count), 1).astype(f32)
    key = jnp.where(place < seen[4:5, :], seen[0:1, :] * rx + cell_x, -1.0)
    flash = seen[2:3, :]
    weight = 1.0 / (seen[3:4, :] * seen[3:4, :])
    for number, value in enumerate((key, cell_y, weight, flash * weight)):
        for part in range(2):
            obs_all[me, 2 * number + part:2 * number + part + 1, :] = value[
                :, part * per:(part + 1) * per
            ]
    start_all(obs_all, obs_s, obs_r)

    raw[...] = jnp.zeros_like(raw)
    raw[:variables, :levels] = rate[0] * (1.0 / (rx * nx))
    raw[variables:2 * variables, :levels] = rate[1] * (1.0 / (ry * ny))
    raw[2 * variables:3 * variables, :levels] = flash_w[...]
    raw[3 * variables:3 * variables + 1, :levels] = level_w[...]
    turned = raw[...].T
    for c in range(3 * variables + 1):
        tab[c] = jnp.broadcast_to(turned[:levels, c:c + 1], (levels, LANES))

    for v in range(variables):
        mine = slice(v * levels, (v + 1) * levels)
        scaled = vert[v] * gain[v:v + 1, :] * tab[2 * variables + v, :, :levels]
        high, low = split(scaled)
        mstack[:levels, mine] = high
        mstack[levels:, mine] = low
        high, low = split((scaled * tab[3 * variables, :, :levels]).T)
        bstack[mine, :levels] = high
        bstack[mine, levels:2 * levels] = high
        bstack[mine, 2 * levels:] = low
    down = lax.broadcasted_iota(jnp.int32, (ry, ry), 0)
    across = lax.broadcasted_iota(jnp.int32, (ry, ry), 1)
    tri[...] = jnp.where(down <= across, 1.0, 0.0).astype(bf16)
    tri_b[...] = jnp.where(down >= across, 1.0, 0.0).astype(bf16)

    def prefix(value, triangle):
        high, low = split(value)
        both = dot(jnp.concatenate([high, low], axis=0), triangle[...])
        return both[:value.shape[0]] + both[value.shape[0]:]

    wide = lambda value: jnp.concatenate([value] * halves, axis=1)
    position = lax.broadcasted_iota(jnp.int32, (8, ry), 1).astype(f32)

    edge[gy] = jnp.zeros((levels, LANES), f32)
    edge_b[gy] = jnp.zeros((levels, LANES), f32)

    @pl.loop(0, variables * tiles, unroll=2)
    def _(i):
        v, tile = i // tiles, lax.rem(i, tiles)
        rows = pl.ds(i * 8, 8)
        sx, sy = rates(v, tile)
        up, fall = jnp.exp(wide(sy) * position), jnp.exp(-wide(sy) * position)
        grow[rows, :], fade[rows, :] = up, fall
        ax = jnp.exp(-sx)
        axt[rows, :] = ax
        ax = wide(ax)
        for h in range(halves):
            stage[v * halves + h] = ctrl[v, pl.ds(tile * 8 * rx, 8 * rx), half(h)]
        parts = [
            jnp.concatenate(
                [stage[v * halves + h, pl.ds(x, 8, stride=rx), :] for h in range(halves)], axis=1
            ) * up
            for x in range(rx)
        ]
        parts = prefix(jnp.concatenate(parts, axis=0), tri)
        state = jnp.zeros((8, ry), f32)
        column = edge[gy, pl.ds(tile * 8, 8), :]
        for x in range(rx):
            part = parts[x * 8:x * 8 + 8] * fall
            last = jnp.broadcast_to(part[:, ry - 1:], (8, LANES))
            column = jnp.where(lane == v * rx + x, last, column)
            state = ax * state + part
            field[x, rows, :] = state
        edge[gy, pl.ds(tile * 8, 8), :] = column

    start_row(edge, e_s, e_r)

    @pl.loop(0, tiles)
    def _(tile):
        for v in range(variables):
            for h in range(halves):
                stage[v * halves + h] = bg[v, pl.ds(tile * 8 * rx, 8 * rx), half(h)]
        weights = [tab[2 * variables + v, pl.ds(tile * 8, 8), :] for v in range(variables)]
        for x in range(rx):
            for h in range(halves):
                part = jnp.zeros((8, LANES), f32)
                for v in range(variables):
                    part = part + weights[v] * stage[v * halves + h, pl.ds(x, 8, stride=rx), :]
                base_levels[x, pl.ds(tile * 8, 8), half(h)] = part

    wait_all(obs_all, obs_s, obs_r)
    sums[...] = jnp.zeros_like(sums)
    row_x = lax.broadcasted_iota(jnp.int32, (rx, per), 0).astype(f32)
    row_y = lax.broadcasted_iota(jnp.int32, (ry, per), 0).astype(f32)
    base = (me * rx).astype(f32)

    @pl.loop(0, devices, unroll=2)
    def _(src):
        total = sums[...]
        for part in range(2):
            key = obs_all[src, part:part + 1, :] - base
            spot = obs_all[src, 2 + part:3 + part, :]
            hit = row_x == key
            pieces = []
            for field_of in (4, 6):
                weight = obs_all[src, field_of + part:field_of + part + 1, :]
                pieces += split(jnp.where(hit, weight, 0.0))
            left = jnp.concatenate(pieces, axis=0)
            right = jnp.where(row_y == spot, 1.0, 0.0).astype(bf16)
            total = total + lax.dot_general(
                right, left, (((1,), (1,)), ((), ())), preferred_element_type=f32
            )
        sums[...] = total

    gathered = sums[...].T
    s1 = gathered[:rx] + gathered[rx:2 * rx]
    s2 = gathered[2 * rx:3 * rx] + gathered[3 * rx:]

    @pl.when(gx == 0)
    def _():
        xin[...] = jnp.zeros_like(xin)

    @pl.when(gx == nx - 1)
    def _():
        xin_b[...] = jnp.zeros_like(xin_b)

    def rates_in_lanes(tile):
        wide = [jnp.zeros((8, LANES), f32)] * 2
        for v in range(variables):
            here = (lane >= v * rx) & (lane < (v + 1) * rx)
            wide = [jnp.where(here, new, old) for new, old in zip(rates(v, tile), wide)]
        return wide

    wait_row(edge, e_s, e_r)

    @pl.loop(0, tiles)
    def _(tile):
        rows = pl.ds(tile * 8, 8)
        sx, sy = rates_in_lanes(tile)
        total = jnp.zeros((8, LANES), f32)
        for src in range(ny):
            far = jnp.maximum(gy - 1 - src, 0).astype(f32) * ry
            total = total + jnp.where(src < gy, jnp.exp(-sy * far) * edge[src, rows, :], 0.0)
        inner = lax.rem(lane, rx)
        s = 1
        while s < rx:
            total = total + jnp.where(inner >= s, jnp.exp(-sx * s), 0.0) * pltpu.roll(total, s, 1)
            s *= 2
        q_ref[rows, :] = total * jnp.exp(-sy)

    for v in range(variables):
        @pl.when(gx > 0)
        def _():
            chain(v, xout, xin, x_s, x_r, gx).wait_recv()

        @pl.when(gx < nx - 1)
        def _():
            @pl.loop(0, tiles)
            def _(tile):
                rows = pl.ds(tile * 8, 8)
                sx, sy = rates(v, tile)
                spot = v * rx + rx - 1
                q = jnp.broadcast_to(q_ref[rows, spot:spot + 1], (8, LANES))
                mine = pl.ds(v * levels + tile * 8, 8)
                xout[v, rows, :] = (
                    field[rx - 1, mine, :] + fade[mine, :] * wide(q)
                    + wide(jnp.exp(-sx * rx)) * xin[v, rows, :]
                )
            chain(v, xout, xin, x_s, x_r, gx + 1).start()

        @pl.loop(0, tiles, unroll=2)
        def _(tile):
            rows = pl.ds(tile * 8, 8)
            mine = pl.ds(v * levels + tile * 8, 8)
            reach = fade[mine, :]
            q_all = q_ref[rows, :]
            ax = wide(axt[mine, :])
            entering = xin[v, rows, :]
            for x in range(rx):
                q = jnp.broadcast_to(q_all[:, v * rx + x:v * rx + x + 1], (8, LANES))
                entering = ax * entering
                field[x, mine, :] = field[x, mine, :] + reach * wide(q) + entering

    def soft_and_slope(value):
        small = jnp.exp(-jnp.abs(value))
        soft = jnp.maximum(value, 0.0) + jnp.log1p(small)
        return soft, jnp.where(value >= 0, 1.0, small) / (1.0 + small)

    @pl.loop(0, rx, unroll=4)
    def _(x):
        high, low = split(field[x])
        both = dot(mstack[...], high)
        value = both[:levels] + both[levels:] + dot(mstack[:levels, :], low) + base_levels[x]
        soft, slope = soft_and_slope(value)
        slopes[x] = slope
        totals[pl.ds(x, 1), :] = jnp.sum(wide(tab[3 * variables]) * soft, axis=0, keepdims=True)

    sp, sg = soft_and_slope(totals[...])
    sp_all[me] = sp
    totals[...] = sg * (sp * s1 - s2)
    start_all(sp_all, sp_s, sp_r)
    row0[...] = jnp.zeros_like(row0)

    @pl.loop(0, rx, unroll=4)
    def _(i):
        x = rx - 1 - i
        high, low = split(totals[pl.ds(x, 1), :] * slopes[x])
        back = dot(bstack[...], jnp.concatenate([high, low, high], axis=0))
        now = wide(axt[...]) * row0[...] + back
        row0[...] = now
        field[x] = now

    for v in range(variables):
        mine = slice(v * levels, (v + 1) * levels)

        @pl.loop(0, rx, unroll=4)
        def _(x):
            field[x, mine, :] = prefix(field[x, mine, :] * fade[mine, :], tri_b) * grow[mine, :]

        @pl.when(gx < nx - 1)
        def _():
            chain(v, xout_b, xin_b, b_s, b_r, gx).wait_recv()

        @pl.when(gx > 0)
        def _():
            xout_b[v] = row0[v * levels:(v + 1) * levels, :] + wide(
                jnp.exp(-tab[v] * rx)
            ) * xin_b[v]
            chain(v, xout_b, xin_b, b_s, b_r, gx - 1).start()

        row0[mine, :] = prefix(xin_b[v] * fade[mine, :], tri_b) * grow[mine, :]

        @pl.loop(0, tiles, unroll=2)
        def _(tile):
            rows = pl.ds(tile * 8, 8)
            here = pl.ds(v * levels + tile * 8, 8)
            ax = axt[here, :]
            first = jnp.broadcast_to(row0[here, :LANES][:, :1], (8, LANES))
            column = edge_b[gy, rows, :]
            for x in range(rx)[::-1]:
                own = field[x, here, :LANES][:, :1]
                first = ax * first
                column = jnp.where(
                    lane == v * rx + x, jnp.broadcast_to(own, (8, LANES)) + first, column
                )
            edge_b[gy, rows, :] = column

    start_row(edge_b, f_s, f_r)

    wait_all(sp_all, sp_s, sp_r)
    column_y = lax.broadcasted_iota(jnp.int32, (ry, count), 0).astype(f32)
    pick = jnp.where(column_y == cell_y, 1.0, 0.0).astype(bf16)
    batch = 8
    row_of = lax.broadcasted_iota(jnp.int32, (batch * rx, count), 0).astype(f32)

    def find(group, found):
        high, low = split(sp_all[pl.ds(group * batch, batch)].reshape(batch * rx, ry))
        value = dot(jnp.concatenate([high, low], axis=0), pick)
        value = value[:batch * rx] + value[batch * rx:]
        hit = row_of == key - (group * (batch * rx)).astype(f32)
        return found + jnp.sum(jnp.where(hit, value, 0.0).reshape(-1, 8, count), axis=0)

    found = lax.fori_loop(0, devices // batch, find, jnp.zeros((8, count), f32))
    found = jnp.sum(found, axis=0, keepdims=True)
    dep[...] = jnp.where(key >= 0, found - flash, 0.0)

    wait_row(edge_b, f_s, f_r)

    @pl.loop(0, tiles)
    def _(tile):
        rows = pl.ds(tile * 8, 8)
        sx, sy = rates_in_lanes(tile)
        total = jnp.zeros((8, LANES), f32)
        for src in range(ny):
            far = jnp.maximum(src - gy - 1, 0).astype(f32) * ry
            total = total + jnp.where(src > gy, jnp.exp(-sy * far) * edge_b[src, rows, :], 0.0)
        total = total * jnp.exp(-sy * ry)
        for v in range(variables):
            mine = pl.ds(v * levels + tile * 8, 8)
            reach = grow[mine, :]
            ax = wide(axt[mine, :])
            entering = row0[mine, :]
            for x in range(rx)[::-1]:
                q = jnp.broadcast_to(total[:, v * rx + x:v * rx + x + 1], (8, LANES))
                entering = ax * entering
                value = field[x, mine, :] + reach * wide(q) + entering
                for h in range(halves):
                    stage[v * halves + h, pl.ds(x, 8, stride=rx), :] = value[:, half(h)]
            for h in range(halves):
                at = (v, pl.ds(tile * 8 * rx, 8 * rx), half(h))
                out[at] = ctrl[at] + stage[v * halves + h]

    for v in range(variables):
        @pl.when(gx < nx - 1)
        def _():
            chain(v, xout, xin, x_s, x_r, gx + 1).wait_send()

        @pl.when(gx > 0)
        def _():
            chain(v, xout_b, xin_b, b_s, b_r, gx - 1).wait_send()


def body(
    control, background, vert_factor, length_rates, flash_weights, level_weights,
    obs_owner, obs_cell, obs_count, flash_obs, obs_error,
):
    variables, levels, rx, ry = control.shape
    nx, ny = lax.axis_size("gx"), lax.axis_size("gy")
    devices = nx * ny
    count = obs_cell.shape[0]
    vk = variables * levels
    step_x = length_rates[0] / (rx * nx)
    step_y = length_rates[1] / (ry * ny)
    gain = jnp.sqrt(jnp.expm1(-2.0 * step_x) * jnp.expm1(-2.0 * step_y))
    limit = jnp.broadcast_to(obs_count, (count,))
    seen = jnp.stack([
        obs_owner[:, 0].astype(f32), obs_cell.astype(f32), flash_obs, obs_error, limit.astype(f32)
    ])

    vmem = pl.BlockSpec(memory_space=pltpu.VMEM)
    dma = pltpu.SemaphoreType.DMA
    grad, departure = pl.pallas_call(
        functools.partial(kernel, nx, ny, variables, levels, rx, ry),
        out_shape=(
            jax.ShapeDtypeStruct((variables, levels * rx, ry), f32),
            jax.ShapeDtypeStruct((1, count), f32),
        ),
        in_specs=[vmem] * 8,
        out_specs=(vmem, vmem),
        scratch_shapes=[
            pltpu.VMEM((rx, vk, ry), f32),
            pltpu.VMEM((ry, 4 * rx), f32),
            pltpu.VMEM((devices, rx, ry), f32),
            pltpu.VMEM((devices, 8, count // 2), f32),
            pltpu.VMEM((ny, levels, LANES), f32),
            pltpu.VMEM((ny, levels, LANES), f32),
            pltpu.VMEM((levels, LANES), f32),
            pltpu.VMEM((variables, levels, ry), f32),
            pltpu.VMEM((variables, levels, ry), f32),
            pltpu.VMEM((variables, levels, ry), f32),
            pltpu.VMEM((variables, levels, ry), f32),
            pltpu.VMEM((vk, ry), f32),
            pltpu.VMEM((vk, LANES), f32),
            pltpu.VMEM((variables * ry // LANES, 8 * rx, LANES), f32),
            pltpu.VMEM((rx, levels, ry), f32),
            pltpu.VMEM((2 * levels, vk), bf16),
            pltpu.VMEM((vk, 3 * levels), bf16),
            pltpu.VMEM((3 * variables + 1, levels, LANES), f32),
            pltpu.VMEM((16, LANES), f32),
            pltpu.VMEM((ry, ry), bf16),
            pltpu.VMEM((ry, ry), bf16),
            pltpu.VMEM((vk, ry), f32),
            pltpu.VMEM((vk, ry), f32),
            pltpu.VMEM((rx, levels, ry), f32),
            pltpu.VMEM((rx, ry), f32),
            dma((devices,)), dma((devices,)), dma((devices,)), dma((devices,)),
            dma((ny,)), dma((ny,)), dma((ny,)), dma((ny,)),
            dma((variables,)), dma((variables,)), dma((variables,)), dma((variables,)),
        ],
        compiler_params=pltpu.CompilerParams(
            collective_id=0, has_side_effects=True, vmem_limit_bytes=48 * 2**20
        ),
    )(
        control.reshape(variables, levels * rx, ry),
        background.reshape(variables, levels * rx, ry),
        vert_factor, length_rates, gain, flash_weights, level_weights[None], seen,
    )
    return grad.reshape(control.shape), departure.reshape(count)


def solution(mesh):
    placed = (
        P(None, None, "gx", "gy"),
        P(None, None, "gx", "gy"),
        P(),
        P(),
        P(),
        P(),
        P(("gx", "gy"), None),
        P(("gx", "gy")),
        P(("gx", "gy")),
        P(("gx", "gy")),
        P(("gx", "gy")),
    )
    return jax.shard_map(
        body,
        mesh=mesh,
        in_specs=placed,
        out_specs=(P(None, None, "gx", "gy"), P(("gx", "gy"))),
        check_vma=False,
    )
```

time: 142 us -> 93.9 us (0.66)
  Pallas kernels: 131 us -> 83.9 us
  other arithmetic: 5.24 us -> 2.08 us
  local copies, waits for them, and re-layouts: 4.52 us -> 6.25 us
    pallas_call x1, Pallas kernels: 131 us -> 83.9 us  [body(): pl.pallas_call(functools.partial(kernel, nx, ny, variables, levels, rx, r...]
    unnamed x2 -> x10, local copies, waits for them, and re-layouts: 2.59 us -> 5.51 us
where the time goes in v1:
time: 93.9 us; the launch traced here: 93.5 us
  Pallas kernels  83.9 us (89%)
  local copies, waits for them, and re-layouts  6.25 us (7%)
  other arithmetic  2.08 us (2%)
  between operations  1.31 us (1%)
    pallas_call x1, Pallas kernels, body(): pl.pallas_call(functools.partial(kernel, nx, ny, variables, levels, rx, r...  83.9 us
    unnamed x10, local copies, waits for them, and re-layouts  5.51 us

profile of v1, /device:TPU:0, one launch (start us, length us, event | category | flops | bytes accessed | tf_op | source)
XLA Modules:
  0.0 93.5 jit_solution(7101095048297825506)
XLA Ops:
  1.3 0.7 convert_bitcast_fusion
  2.0 0.7 convert_element_type.25
  2.7 0.7 sqrt_bitcast_fusion.gain
  3.4 0.7 stack.20.seen
  4.1 0.0 copy-start
  4.1 0.9 copy-done
  5.0 0.0 copy-start.1
  5.0 0.7 copy-done.1
  5.7 0.0 copy-start.2
  5.7 0.7 copy-done.2
  6.4 0.0 copy-start.3
  6.4 0.7 copy-done.3
  7.0 83.9 %shard_map.122 = (f32[4,1024,256]{2,1,0:T(8,128)S(1)}, f32[1,512]{1,0:T(1,128)S(1)}) custom-call(f32[4,1024,256]{2,1,0:T(8,128)} %bitcast.16, f32[4,1024,256]{2,1,0:T(8,128)} %bitcast.17, f32[4,64,64]{2,1,0:T(8,128)S(1)} %copy-done, f32[2,4,64]{2,1,0:T(4,128)S(1)} %copy-done.1, f32[4,64]{1,0:T(4,128)S(1)} %sqrt_bitcast_fusion.gain, f32[4,64]{1,0:T(4,128)S(1)} %copy-done.2, ...), custom_call_target="tpu_custom_call" | custom-call | tf_op jit(solution)/shard_map/pallas_call | solution.py:427
  90.9 2.0 %copy.16 = f32[4,64,16,256]{3,2,1,0:T(8,128)} copy(f32[4,64,16,256]{3,2,1,0:T(8,128)S(1)} %bitcast.13) | data formatting | bytes 8388608
  93.0 0.6 copy.17
  (1 shorter events, 0.0 us)
Async XLA Ops:
  4.1 0.9 copy-start
  5.0 0.7 copy-start.1
  5.7 0.7 copy-start.2
  6.4 0.7 copy-start.3

commit v2 on v1

--- a/solution.py
+++ b/solution.py
@@ -22,10 +22,12 @@
 
 def kernel(
     nx, ny, variables, levels, rx, ry,
-    ctrl, bg, vert, rate, gain, flash_w, level_w, seen,
+    gain, ctrl_h, bg_h, vert_h, rate_h, flash_w_h, level_w_h, owner_h, cell_h, seen_h, error_h, live_h,
     out, dep,
     field, sums, sp_all, obs_all, edge, edge_b, q_ref, xin, xout, xin_b, xout_b, row0, axt, stage,
     base_levels, mstack, bstack, tab, raw, tri, tri_b, grow, fade, slopes, totals,
+    qx, bx, ctrl, bg, vert, rate, flash_w, level_w, owner, cell, seen, error, live,
+    in_s, ctrl_s, qx_s, qx_r, bx_s, bx_r,
     obs_s, obs_r, sp_s, sp_r, e_s, e_r, f_s, f_r, x_s, x_r, b_s, b_r,
 ):
     devices = nx * ny
@@ -35,6 +37,18 @@
     tiles = levels // 8
     vk = variables * levels
     lane = lax.broadcasted_iota(jnp.int32, (8, LANES), 1)
+    small = [
+        (vert_h, vert), (rate_h, rate), (flash_w_h, flash_w), (level_w_h, level_w),
+        (owner_h, owner), (cell_h, cell), (seen_h, seen), (error_h, error), (live_h, live),
+    ]
+    small = [pltpu.make_async_copy(a, b, in_s.at[i + 1]) for i, (a, b) in enumerate(small)]
+    bg_copy = pltpu.make_async_copy(bg_h, bg, in_s.at[0])
+    ctrl_copy = [
+        pltpu.make_async_copy(ctrl_h.at[v], ctrl.at[v], ctrl_s.at[v]) for v in range(variables)
+    ]
+    for copy in small + ctrl_copy + [bg_copy]:
+        copy.start()
+
     def peer(offset):
         other = lax.rem(me + offset, devices)
         return (other // ny, lax.rem(other, ny))
@@ -97,16 +111,19 @@
     @pl.loop(1, devices)
     def _(offset):
         pl.semaphore_signal(barrier, inc=1, device_id=peer(offset), device_id_type=MESH)
+    for copy in small:
+        copy.wait()
     pl.semaphore_wait(barrier, devices - 1)
 
     count = seen.shape[1]
     per = count // 2
-    cell_x = jnp.floor(seen[1:2, :] * (1.0 / ry))
-    cell_y = seen[1:2, :] - cell_x * ry
-    place = lax.broadcasted_iota(jnp.int32, (1, count), 1).astype(f32)
-    key = jnp.where(place < seen[4:5, :], seen[0:1, :] * rx + cell_x, -1.0)
-    flash = seen[2:3, :]
-    weight = 1.0 / (seen[3:4, :] * seen[3:4, :])
+    where = cell[...].astype(f32)
+    cell_x = jnp.floor(where * (1.0 / ry))
+    cell_y = where - cell_x * ry
+    place = lax.broadcasted_iota(jnp.int32, (1, count), 1)
+    key = jnp.where(place < live[...], owner[...].astype(f32) * rx + cell_x, -1.0)
+    flash = seen[...]
+    weight = 1.0 / (error[...] * error[...])
     for number, value in enumerate((key, cell_y, weight, flash * weight)):
         for part in range(2):
             obs_all[me, 2 * number + part:2 * number + part + 1, :] = value[
@@ -147,38 +164,121 @@
     position = lax.broadcasted_iota(jnp.int32, (8, ry), 1).astype(f32)
 
     edge[gy] = jnp.zeros((levels, LANES), f32)
-    edge_b[gy] = jnp.zeros((levels, LANES), f32)
-
-    @pl.loop(0, variables * tiles, unroll=2)
-    def _(i):
-        v, tile = i // tiles, lax.rem(i, tiles)
-        rows = pl.ds(i * 8, 8)
-        sx, sy = rates(v, tile)
-        up, fall = jnp.exp(wide(sy) * position), jnp.exp(-wide(sy) * position)
-        grow[rows, :], fade[rows, :] = up, fall
-        ax = jnp.exp(-sx)
-        axt[rows, :] = ax
-        ax = wide(ax)
-        for h in range(halves):
-            stage[v * halves + h] = ctrl[v, pl.ds(tile * 8 * rx, 8 * rx), half(h)]
-        parts = [
-            jnp.concatenate(
-                [stage[v * halves + h, pl.ds(x, 8, stride=rx), :] for h in range(halves)], axis=1
-            ) * up
-            for x in range(rx)
-        ]
-        parts = prefix(jnp.concatenate(parts, axis=0), tri)
-        state = jnp.zeros((8, ry), f32)
-        column = edge[gy, pl.ds(tile * 8, 8), :]
-        for x in range(rx):
-            part = parts[x * 8:x * 8 + 8] * fall
-            last = jnp.broadcast_to(part[:, ry - 1:], (8, LANES))
-            column = jnp.where(lane == v * rx + x, last, column)
-            state = ax * state + part
-            field[x, rows, :] = state
-        edge[gy, pl.ds(tile * 8, 8), :] = column
-
-    start_row(edge, e_s, e_r)
+    bx[gx] = jnp.zeros((levels, LANES), f32)
+
+    @pl.when(gx == 0)
+    def _():
+        xin[...] = jnp.zeros_like(xin)
+
+    @pl.when(gx == nx - 1)
+    def _():
+        xin_b[...] = jnp.zeros_like(xin_b)
+
+    def step(slot, lag, last, next_x, own, source, target, send, recv):
+        v = slot - lag
+
+        @pl.when((v >= 0) & (v < variables))
+        def _():
+            @pl.when(lag > 0)
+            def _():
+                chain(v, source, target, send, recv, gx).wait_recv()
+
+            @pl.when(lag < last)
+            def _():
+                source[v] = own(pl.ds(v * levels, levels)) + wide(
+                    jnp.exp(-tab[v] * rx)
+                ) * target[v]
+                chain(v, source, target, send, recv, next_x).start()
+
+    def step_forward(slot):
+        step(slot, gx, nx - 1, gx + 1, lambda rows: field[rx - 1, rows, :], xout, xin, x_s, x_r)
+
+    def step_back(slot):
+        step(slot, nx - 1 - gx, nx - 1, gx - 1, lambda rows: row0[rows, :], xout_b, xin_b, b_s, b_r)
+
+    slots = variables + nx - 1
+
+    def corner(ref, send, recv, other, slot):
+        return pltpu.make_async_remote_copy(
+            ref.at[slot], ref.at[slot], send.at[other], recv.at[slot], (other, gy), MESH
+        )
+
+    def start_corner(ref, send, recv, ahead):
+        for other in range(nx):
+            @pl.when(ahead(gx, other))
+            def _():
+                corner(ref, send, recv, other, gx).start()
+
+    def wait_corner(ref, send, recv, ahead):
+        for other in range(nx):
+            @pl.when(ahead(other, gx))
+            def _():
+                corner(ref, send, recv, other, other).wait_recv()
+
+            @pl.when(ahead(gx, other))
+            def _():
+                corner(ref, send, recv, other, gx).wait_send()
+
+    later, sooner = lambda a, b: b > a, lambda a, b: b < a
+    inner = lax.rem(lane, rx)
+
+    def scan_x(total, sx):
+        s = 1
+        while s < rx:
+            total = total + jnp.where(inner >= s, jnp.exp(-sx * s), 0.0) * pltpu.roll(total, s, 1)
+            s *= 2
+        return total
+
+    def rates_in_lanes(tile):
+        both = [jnp.zeros((8, LANES), f32)] * 2
+        for v in range(variables):
+            here = (lane >= v * rx) & (lane < (v + 1) * rx)
+            both = [jnp.where(here, new, old) for new, old in zip(rates(v, tile), both)]
+        return both
+
+    for v in range(variables):
+        ctrl_copy[v].wait()
+
+        @pl.loop(0, tiles // 2)
+        def _(pair):
+            parts, falls, decays = [], [], []
+            for k in range(2):
+                tile = pair * 2 + k
+                rows = pl.ds(v * levels + tile * 8, 8)
+                sx, sy = rates(v, tile)
+                up, fall = jnp.exp(wide(sy) * position), jnp.exp(-wide(sy) * position)
+                grow[rows, :], fade[rows, :] = up, fall
+                ax = jnp.exp(-sx)
+                axt[rows, :] = ax
+                falls.append(fall)
+                decays.append(wide(ax))
+                for h in range(halves):
+                    stage[k * halves + h] = ctrl[v, pl.ds(tile * 8 * rx, 8 * rx), half(h)]
+                for x in range(rx):
+                    strips = [
+                        stage[k * halves + h, pl.ds(x, 8, stride=rx), :] for h in range(halves)
+                    ]
+                    parts.append(jnp.concatenate(strips, axis=1) * up)
+            parts = prefix(jnp.concatenate(parts, axis=0), tri)
+            for k in range(2):
+                tile = pair * 2 + k
+                rows = pl.ds(v * levels + tile * 8, 8)
+                state = jnp.zeros((8, ry), f32)
+                column = edge[gy, pl.ds(tile * 8, 8), :]
+                for x in range(rx):
+                    at = (k * rx + x) * 8
+                    part = parts[at:at + 8] * falls[k]
+                    last = jnp.broadcast_to(part[:, ry - 1:], (8, LANES))
+                    column = jnp.where(lane == v * rx + x, last, column)
+                    state = decays[k] * state + part
+                    field[x, rows, :] = state
+                edge[gy, pl.ds(tile * 8, 8), :] = column
+
+        if v == variables - 1:
+            start_row(edge, e_s, e_r)
+        step_forward(v)
+
+    bg_copy.wait()
 
     @pl.loop(0, tiles)
     def _(tile):
@@ -193,6 +293,7 @@
                     part = part + weights[v] * stage[v * halves + h, pl.ds(x, 8, stride=rx), :]
                 base_levels[x, pl.ds(tile * 8, 8), half(h)] = part
 
+    step_forward(variables)
     wait_all(obs_all, obs_s, obs_r)
     sums[...] = jnp.zeros_like(sums)
     row_x = lax.broadcasted_iota(jnp.int32, (rx, per), 0).astype(f32)
@@ -201,41 +302,26 @@
 
     @pl.loop(0, devices, unroll=2)
     def _(src):
-        total = sums[...]
+        pieces, rights = [], []
         for part in range(2):
-            key = obs_all[src, part:part + 1, :] - base
+            hit = row_x == obs_all[src, part:part + 1, :] - base
             spot = obs_all[src, 2 + part:3 + part, :]
-            hit = row_x == key
-            pieces = []
+            rows = []
             for field_of in (4, 6):
-                weight = obs_all[src, field_of + part:field_of + part + 1, :]
-                pieces += split(jnp.where(hit, weight, 0.0))
-            left = jnp.concatenate(pieces, axis=0)
-            right = jnp.where(row_y == spot, 1.0, 0.0).astype(bf16)
-            total = total + lax.dot_general(
-                right, left, (((1,), (1,)), ((), ())), preferred_element_type=f32
-            )
-        sums[...] = total
+                load = obs_all[src, field_of + part:field_of + part + 1, :]
+                rows += split(jnp.where(hit, load, 0.0))
+            pieces.append(jnp.concatenate(rows, axis=0))
+            rights.append(jnp.where(row_y == spot, 1.0, 0.0).astype(bf16))
+        sums[...] += lax.dot_general(
+            jnp.concatenate(rights, axis=1), jnp.concatenate(pieces, axis=1),
+            (((1,), (1,)), ((), ())), preferred_element_type=f32,
+        )
 
     gathered = sums[...].T
     s1 = gathered[:rx] + gathered[rx:2 * rx]
     s2 = gathered[2 * rx:3 * rx] + gathered[3 * rx:]
 
-    @pl.when(gx == 0)
-    def _():
-        xin[...] = jnp.zeros_like(xin)
-
-    @pl.when(gx == nx - 1)
-    def _():
-        xin_b[...] = jnp.zeros_like(xin_b)
-
-    def rates_in_lanes(tile):
-        wide = [jnp.zeros((8, LANES), f32)] * 2
-        for v in range(variables):
-            here = (lane >= v * rx) & (lane < (v + 1) * rx)
-            wide = [jnp.where(here, new, old) for new, old in zip(rates(v, tile), wide)]
-        return wide
-
+    step_forward(variables + 1)
     wait_row(edge, e_s, e_r)
 
     @pl.loop(0, tiles)
@@ -246,33 +332,27 @@
         for src in range(ny):
             far = jnp.maximum(gy - 1 - src, 0).astype(f32) * ry
             total = total + jnp.where(src < gy, jnp.exp(-sy * far) * edge[src, rows, :], 0.0)
-        inner = lax.rem(lane, rx)
-        s = 1
-        while s < rx:
-            total = total + jnp.where(inner >= s, jnp.exp(-sx * s), 0.0) * pltpu.roll(total, s, 1)
-            s *= 2
-        q_ref[rows, :] = total * jnp.exp(-sy)
+        q_ref[rows, :] = total
+        qx[gx, rows, :] = scan_x(total, sx)
+
+    start_corner(qx, qx_s, qx_r, later)
+    for slot in range(variables + 2, slots):
+        step_forward(slot)
+    wait_corner(qx, qx_s, qx_r, later)
+
+    @pl.loop(0, tiles)
+    def _(tile):
+        rows = pl.ds(tile * 8, 8)
+        sx, sy = rates_in_lanes(tile)
+        total = jnp.zeros((8, LANES), f32)
+        for src in range(nx):
+            far = jnp.maximum(gx - 1 - src, 0).astype(f32) * rx
+            total = total + jnp.where(src < gx, jnp.exp(-sx * far) * qx[src, rows, :], 0.0)
+        total = jnp.exp(-sx) * pltpu.roll(total, LANES - (rx - 1), 1)
+        total = q_ref[rows, :] + jnp.where(inner == 0, total, 0.0)
+        q_ref[rows, :] = scan_x(total, sx) * jnp.exp(-sy)
 
     for v in range(variables):
-        @pl.when(gx > 0)
-        def _():
-            chain(v, xout, xin, x_s, x_r, gx).wait_recv()
-
-        @pl.when(gx < nx - 1)
-        def _():
-            @pl.loop(0, tiles)
-            def _(tile):
-                rows = pl.ds(tile * 8, 8)
-                sx, sy = rates(v, tile)
-                spot = v * rx + rx - 1
-                q = jnp.broadcast_to(q_ref[rows, spot:spot + 1], (8, LANES))
-                mine = pl.ds(v * levels + tile * 8, 8)
-                xout[v, rows, :] = (
-                    field[rx - 1, mine, :] + fade[mine, :] * wide(q)
-                    + wide(jnp.exp(-sx * rx)) * xin[v, rows, :]
-                )
-            chain(v, xout, xin, x_s, x_r, gx + 1).start()
-
         @pl.loop(0, tiles, unroll=2)
         def _(tile):
             rows = pl.ds(tile * 8, 8)
@@ -318,40 +398,46 @@
     for v in range(variables):
         mine = slice(v * levels, (v + 1) * levels)
 
-        @pl.loop(0, rx, unroll=4)
-        def _(x):
-            field[x, mine, :] = prefix(field[x, mine, :] * fade[mine, :], tri_b) * grow[mine, :]
-
-        @pl.when(gx < nx - 1)
-        def _():
-            chain(v, xout_b, xin_b, b_s, b_r, gx).wait_recv()
-
-        @pl.when(gx > 0)
-        def _():
-            xout_b[v] = row0[v * levels:(v + 1) * levels, :] + wide(
-                jnp.exp(-tab[v] * rx)
-            ) * xin_b[v]
-            chain(v, xout_b, xin_b, b_s, b_r, gx - 1).start()
-
-        row0[mine, :] = prefix(xin_b[v] * fade[mine, :], tri_b) * grow[mine, :]
+        @pl.loop(0, rx // 4)
+        def _(group):
+            lag, lead = fade[mine, :][None], grow[mine, :][None]
+            value = field[pl.ds(group * 4, 4), mine, :] * lag
+            value = prefix(value.reshape(4 * levels, ry), tri_b).reshape(4, levels, ry)
+            field[pl.ds(group * 4, 4), mine, :] = value * lead
 
         @pl.loop(0, tiles, unroll=2)
         def _(tile):
             rows = pl.ds(tile * 8, 8)
             here = pl.ds(v * levels + tile * 8, 8)
-            ax = axt[here, :]
-            first = jnp.broadcast_to(row0[here, :LANES][:, :1], (8, LANES))
-            column = edge_b[gy, rows, :]
-            for x in range(rx)[::-1]:
+            column = bx[gx, rows, :]
+            for x in range(rx):
                 own = field[x, here, :LANES][:, :1]
-                first = ax * first
-                column = jnp.where(
-                    lane == v * rx + x, jnp.broadcast_to(own, (8, LANES)) + first, column
-                )
-            edge_b[gy, rows, :] = column
+                column = jnp.where(lane == v * rx + x, jnp.broadcast_to(own, (8, LANES)), column)
+            bx[gx, rows, :] = column
+
+        if v == variables - 1:
+            start_corner(bx, bx_s, bx_r, sooner)
+        step_back(v)
+
+    wait_corner(bx, bx_s, bx_r, sooner)
+
+    @pl.loop(0, tiles)
+    def _(tile):
+        rows = pl.ds(tile * 8, 8)
+        sx, sy = rates_in_lanes(tile)
+        total = jnp.zeros((8, LANES), f32)
+        for src in range(nx):
+            far = jnp.maximum(src - gx - 1, 0).astype(f32) * rx
+            total = total + jnp.where(src > gx, jnp.exp(-sx * far) * bx[src, rows, :], 0.0)
+        total = jnp.where(inner == 0, total, 0.0)
+        s = 1
+        while s < rx:
+            total = total + jnp.where((inner >= s) & (inner < 2 * s), pltpu.roll(total, s, 1), 0.0)
+            s *= 2
+        edge_b[gy, rows, :] = bx[gx, rows, :] + jnp.exp(-sx * (rx - inner).astype(f32)) * total
 
     start_row(edge_b, f_s, f_r)
-
+    step_back(variables)
     wait_all(sp_all, sp_s, sp_r)
     column_y = lax.broadcasted_iota(jnp.int32, (ry, count), 0).astype(f32)
     pick = jnp.where(column_y == cell_y, 1.0, 0.0).astype(bf16)
@@ -369,6 +455,10 @@
     found = jnp.sum(found, axis=0, keepdims=True)
     dep[...] = jnp.where(key >= 0, found - flash, 0.0)
 
+    for slot in range(variables + 1, slots):
+        step_back(slot)
+    entered = xin_b[...].reshape(vk, ry) * fade[...]
+    row0[...] = prefix(entered, tri_b) * grow[...]
     wait_row(edge_b, f_s, f_r)
 
     @pl.loop(0, tiles)
@@ -417,11 +507,6 @@
     step_x = length_rates[0] / (rx * nx)
     step_y = length_rates[1] / (ry * ny)
     gain = jnp.sqrt(jnp.expm1(-2.0 * step_x) * jnp.expm1(-2.0 * step_y))
-    limit = jnp.broadcast_to(obs_count, (count,))
-    seen = jnp.stack([
-        obs_owner[:, 0].astype(f32), obs_cell.astype(f32), flash_obs, obs_error, limit.astype(f32)
-    ])
-
     vmem = pl.BlockSpec(memory_space=pltpu.VMEM)
     dma = pltpu.SemaphoreType.DMA
     grad, departure = pl.pallas_call(
@@ -430,7 +515,7 @@
             jax.ShapeDtypeStruct((variables, levels * rx, ry), f32),
             jax.ShapeDtypeStruct((1, count), f32),
         ),
-        in_specs=[vmem] * 8,
+        in_specs=[vmem] + [pl.BlockSpec(memory_space=pltpu.HBM)] * 11,
         out_specs=(vmem, vmem),
         scratch_shapes=[
             pltpu.VMEM((rx, vk, ry), f32),
@@ -458,17 +543,32 @@
             pltpu.VMEM((vk, ry), f32),
             pltpu.VMEM((rx, levels, ry), f32),
             pltpu.VMEM((rx, ry), f32),
+            pltpu.VMEM((nx, levels, LANES), f32),
+            pltpu.VMEM((nx, levels, LANES), f32),
+            pltpu.VMEM((variables, levels * rx, ry), f32),
+            pltpu.VMEM((variables, levels * rx, ry), f32),
+            pltpu.VMEM((variables, levels, levels), f32),
+            pltpu.VMEM((2, variables, levels), f32),
+            pltpu.VMEM((variables, levels), f32),
+            pltpu.VMEM((1, levels), f32),
+            pltpu.VMEM((1, count), jnp.int32),
+            pltpu.VMEM((1, count), jnp.int32),
+            pltpu.VMEM((1, count), f32),
+            pltpu.VMEM((1, count), f32),
+            pltpu.VMEM((1, 1), jnp.int32),
+            dma((10,)), dma((variables,)), dma((nx,)), dma((nx,)), dma((nx,)), dma((nx,)),
             dma((devices,)), dma((devices,)), dma((devices,)), dma((devices,)),
             dma((ny,)), dma((ny,)), dma((ny,)), dma((ny,)),
             dma((variables,)), dma((variables,)), dma((variables,)), dma((variables,)),
         ],
         compiler_params=pltpu.CompilerParams(
-            collective_id=0, has_side_effects=True, vmem_limit_bytes=48 * 2**20
+            collective_id=0, has_side_effects=True, vmem_limit_bytes=58 * 2**20
         ),
     )(
-        control.reshape(variables, levels * rx, ry),
+        gain, control.reshape(variables, levels * rx, ry),
         background.reshape(variables, levels * rx, ry),
-        vert_factor, length_rates, gain, flash_weights, level_weights[None], seen,
+        vert_factor, length_rates, flash_weights, level_weights[None], obs_owner.reshape(1, count),
+        obs_cell[None], flash_obs[None], obs_error[None], obs_count[None],
     )
     return grad.reshape(control.shape), departure.reshape(count)
 

time: 93.9 us -> 81.6 us (0.87)
  Pallas kernels: 83.9 us -> 73.6 us
  local copies, waits for them, and re-layouts: 6.25 us -> 5.22 us
    pallas_call x1, Pallas kernels: 83.9 us -> 73.6 us  [body(): pl.pallas_call(functools.partial(kernel, nx, ny, variables, levels, rx, r...]
    convert_element_type x2 -> x0, other arithmetic: 1.37 us -> none  [the longest x1 0.69 us: body(): obs_owner[:, 0].astype(f32)]
    unnamed x10 -> x4, local copies, waits for them, and re-layouts: 5.51 us -> 5.22 us
where the time goes in v2:
time: 81.6 us; the launch traced here: 81.4 us
  Pallas kernels  73.6 us (90%)
  local copies, waits for them, and re-layouts  5.22 us (6%)
  other arithmetic  1.3 us (2%)
  between operations  1.29 us (2%)
    pallas_call x1, Pallas kernels, body(): pl.pallas_call(functools.partial(kernel, nx, ny, variables, levels, rx, r...  73.6 us
    unnamed x4, local copies, waits for them, and re-layouts  5.22 us

profile of v2, /device:TPU:0, one launch (start us, length us, event | category | flops | bytes accessed | tf_op | source)
XLA Modules:
  0.0 81.4 jit_solution(15930035784731264802)
XLA Ops:
  1.3 1.3 %sqrt_bitcast_fusion.gain = f32[4,64]{1,0:T(4,128)} fusion(f32[2,4,64]{2,1,0:T(4,128)} %rate_h.1), kind=kLoop, calls=%fused_computation | loop fusion | flops 768 | bytes 3072 | tf_op jit(solution)/shard_map/sqrt | solution.py:509
  2.6 73.6 %shard_map.122 = (f32[4,1024,256]{2,1,0:T(8,128)}, f32[1,512]{1,0:T(1,128)}) custom-call(f32[4,64]{1,0:T(4,128)} %sqrt_bitcast_fusion.gain, f32[4,1024,256]{2,1,0:T(8,128)} %bitcast.13, f32[4,1024,256]{2,1,0:T(8,128)} %bitcast.14, f32[4,64,64]{2,1,0:T(8,128)} %vert_h.1, f32[2,4,64]{2,1,0:T(4,128)} %rate_h.1, f32[4,64]{1,0:T(4,128)} %flash_w_h.1, ...), custom_call_target="tpu_custom_call" | custom-call | tf_op jit(solution)/shard_map/pallas_call | solution.py:512
  76.2 0.0 copy-start
  76.2 4.6 %copy.16 = f32[4,64,16,256]{3,2,1,0:T(8,128)} copy(f32[4,64,16,256]{3,2,1,0:T(8,128)} %bitcast.15) | data formatting | bytes 8388608
  80.8 0.0 copy-done
  80.8 0.6 copy.17
Async XLA Ops:
  76.2 4.7 %copy-start = (f32[1,512]{1,0:T(1,128)S(1)}, f32[1,512]{1,0:T(1,128)}, u32[]{:S(2)}) copy-start(f32[1,512]{1,0:T(1,128)} %get-tuple-element.5) | copy-start | bytes 6148

commit v3 on v2

--- a/solution.py
+++ b/solution.py
@@ -23,9 +23,9 @@
 def kernel(
     nx, ny, variables, levels, rx, ry,
     gain, ctrl_h, bg_h, vert_h, rate_h, flash_w_h, level_w_h, owner_h, cell_h, seen_h, error_h, live_h,
-    out, dep,
-    field, sums, sp_all, obs_all, edge, edge_b, q_ref, xin, xout, xin_b, xout_b, row0, axt, stage,
-    base_levels, mstack, bstack, tab, raw, tri, tri_b, grow, fade, slopes, totals,
+    field, row0, grow, axt, ending, dep,
+    sums, sp_all, obs_all, edge, edge_b, q_ref, xin, xout, xin_b, xout_b, stage,
+    base_levels, mstack, bstack, tab, raw, tri, tri_b, fade, slopes, totals,
     qx, bx, ctrl, bg, vert, rate, flash_w, level_w, owner, cell, seen, error, live,
     in_s, ctrl_s, qx_s, qx_r, bx_s, bx_r,
     obs_s, obs_r, sp_s, sp_r, e_s, e_r, f_s, f_r, x_s, x_r, b_s, b_r,
@@ -113,7 +113,6 @@
         pl.semaphore_signal(barrier, inc=1, device_id=peer(offset), device_id_type=MESH)
     for copy in small:
         copy.wait()
-    pl.semaphore_wait(barrier, devices - 1)
 
     count = seen.shape[1]
     per = count // 2
@@ -129,7 +128,6 @@
             obs_all[me, 2 * number + part:2 * number + part + 1, :] = value[
                 :, part * per:(part + 1) * per
             ]
-    start_all(obs_all, obs_s, obs_r)
 
     raw[...] = jnp.zeros_like(raw)
     raw[:variables, :levels] = rate[0] * (1.0 / (rx * nx))
@@ -274,6 +272,9 @@
                     field[x, rows, :] = state
                 edge[gy, pl.ds(tile * 8, 8), :] = column
 
+        if v == 0:
+            pl.semaphore_wait(barrier, devices - 1)
+            start_all(obs_all, obs_s, obs_r)
         if v == variables - 1:
             start_row(edge, e_s, e_r)
         step_forward(v)
@@ -469,21 +470,7 @@
         for src in range(ny):
             far = jnp.maximum(src - gy - 1, 0).astype(f32) * ry
             total = total + jnp.where(src > gy, jnp.exp(-sy * far) * edge_b[src, rows, :], 0.0)
-        total = total * jnp.exp(-sy * ry)
-        for v in range(variables):
-            mine = pl.ds(v * levels + tile * 8, 8)
-            reach = grow[mine, :]
-            ax = wide(axt[mine, :])
-            entering = row0[mine, :]
-            for x in range(rx)[::-1]:
-                q = jnp.broadcast_to(total[:, v * rx + x:v * rx + x + 1], (8, LANES))
-                entering = ax * entering
-                value = field[x, mine, :] + reach * wide(q) + entering
-                for h in range(halves):
-                    stage[v * halves + h, pl.ds(x, 8, stride=rx), :] = value[:, half(h)]
-            for h in range(halves):
-                at = (v, pl.ds(tile * 8 * rx, 8 * rx), half(h))
-                out[at] = ctrl[at] + stage[v * halves + h]
+        ending[rows, :] = total * jnp.exp(-sy * ry)
 
     for v in range(variables):
         @pl.when(gx < nx - 1)
@@ -493,6 +480,33 @@
         @pl.when(gx > 0)
         def _():
             chain(v, xout_b, xin_b, b_s, b_r, gx - 1).wait_send()
+
+
+def assemble(variables, rx, ctrl, field, row0, grow, axt, ending, out, stage):
+    halves = out.shape[2] // LANES
+    v = pl.program_id(0)
+    for tile in range(field.shape[1] // 8):
+        rows = slice(tile * 8, tile * 8 + 8)
+        block = slice(tile * 8 * rx, (tile + 1) * 8 * rx)
+        total = ending[rows, :]
+        moved = jnp.zeros_like(total)
+        for number in range(variables):
+            part = total if number == 0 else pltpu.roll(total, LANES - number * rx, 1)
+            moved = jnp.where(v == number, part, moved)
+        ax = jnp.concatenate([axt[rows, :]] * halves, axis=1)
+        entering = row0[rows, :]
+        for x in range(rx)[::-1]:
+            q = jnp.broadcast_to(moved[:, x:x + 1], (8, LANES))
+            entering = ax * entering
+            value = field[x, rows, :] + grow[rows, :] * jnp.concatenate([q] * halves, axis=1)
+            value = value + entering
+            for h in range(halves):
+                stage[tile * halves + h, pl.ds(x, 8, stride=rx), :] = value[
+                    :, h * LANES:(h + 1) * LANES
+                ]
+        for h in range(halves):
+            lanes = slice(h * LANES, (h + 1) * LANES)
+            out[0, block, lanes] = ctrl[0, block, lanes] + stage[tile * halves + h]
 
 
 def body(
@@ -509,16 +523,19 @@
     gain = jnp.sqrt(jnp.expm1(-2.0 * step_x) * jnp.expm1(-2.0 * step_y))
     vmem = pl.BlockSpec(memory_space=pltpu.VMEM)
     dma = pltpu.SemaphoreType.DMA
-    grad, departure = pl.pallas_call(
+    field, row0, grow, axt, ending, departure = pl.pallas_call(
         functools.partial(kernel, nx, ny, variables, levels, rx, ry),
         out_shape=(
-            jax.ShapeDtypeStruct((variables, levels * rx, ry), f32),
+            jax.ShapeDtypeStruct((rx, vk, ry), f32),
+            jax.ShapeDtypeStruct((vk, ry), f32),
+            jax.ShapeDtypeStruct((vk, ry), f32),
+            jax.ShapeDtypeStruct((vk, LANES), f32),
+            jax.ShapeDtypeStruct((levels, LANES), f32),
             jax.ShapeDtypeStruct((1, count), f32),
         ),
         in_specs=[vmem] + [pl.BlockSpec(memory_space=pltpu.HBM)] * 11,
-        out_specs=(vmem, vmem),
+        out_specs=(vmem,) * 6,
         scratch_shapes=[
-            pltpu.VMEM((rx, vk, ry), f32),
             pltpu.VMEM((ry, 4 * rx), f32),
             pltpu.VMEM((devices, rx, ry), f32),
             pltpu.VMEM((devices, 8, count // 2), f32),
@@ -529,8 +546,6 @@
             pltpu.VMEM((variables, levels, ry), f32),
             pltpu.VMEM((variables, levels, ry), f32),
             pltpu.VMEM((variables, levels, ry), f32),
-            pltpu.VMEM((vk, ry), f32),
-            pltpu.VMEM((vk, LANES), f32),
             pltpu.VMEM((variables * ry // LANES, 8 * rx, LANES), f32),
             pltpu.VMEM((rx, levels, ry), f32),
             pltpu.VMEM((2 * levels, vk), bf16),
@@ -539,7 +554,6 @@
             pltpu.VMEM((16, LANES), f32),
             pltpu.VMEM((ry, ry), bf16),
             pltpu.VMEM((ry, ry), bf16),
-            pltpu.VMEM((vk, ry), f32),
             pltpu.VMEM((vk, ry), f32),
             pltpu.VMEM((rx, levels, ry), f32),
             pltpu.VMEM((rx, ry), f32),
@@ -570,6 +584,26 @@
         vert_factor, length_rates, flash_weights, level_weights[None], obs_owner.reshape(1, count),
         obs_cell[None], flash_obs[None], obs_error[None], obs_count[None],
     )
+    cuts = 2
+    deep = levels // cuts
+    rows_at = lambda v, c: (v * cuts + c, 0)
+    whole = pl.BlockSpec((1, deep * rx, ry), lambda v, c: (v, c, 0))
+    grad = pl.pallas_call(
+        functools.partial(assemble, variables, rx),
+        grid=(variables, cuts),
+        out_shape=jax.ShapeDtypeStruct((variables, levels * rx, ry), f32),
+        in_specs=[
+            whole,
+            pl.BlockSpec((rx, deep, ry), lambda v, c: (0, v * cuts + c, 0)),
+            pl.BlockSpec((deep, ry), rows_at),
+            pl.BlockSpec((deep, ry), rows_at),
+            pl.BlockSpec((deep, LANES), rows_at),
+            pl.BlockSpec((deep, LANES), lambda v, c: (c, 0)),
+        ],
+        out_specs=whole,
+        scratch_shapes=[pltpu.VMEM((deep // 8 * ry // LANES, 8 * rx, LANES), f32)],
+        compiler_params=pltpu.CompilerParams(vmem_limit_bytes=58 * 2**20),
+    )(control.reshape(variables, levels * rx, ry), field, row0, grow, axt, ending)
     return grad.reshape(control.shape), departure.reshape(count)
 
 

time: 81.6 us -> 83.4 us (1.022)
  Pallas kernels: 73.6 us -> 79.9 us
  local copies, waits for them, and re-layouts: 5.22 us -> 0.58 us
    pallas_call x0 -> x1, Pallas kernels: none -> 8.73 us  [body(): pl.pallas_call(functools.partial(assemble, variables, rx), grid=(variable...]
    unnamed x4 -> x3, local copies, waits for them, and re-layouts: 5.22 us -> 0.58 us
    pallas_call x1, Pallas kernels: 73.6 us -> 71.1 us  [body(): pl.pallas_call(functools.partial(kernel, nx, ny, variables, levels, rx, r...]
where the time goes in v3:
time: 83.4 us; the launch traced here: 83 us
  Pallas kernels  79.9 us (96%)
  other arithmetic  1.3 us (2%)
  between operations  1.29 us (2%)
    pallas_call x1, Pallas kernels, body(): pl.pallas_call(functools.partial(kernel, nx, ny, variables, levels, rx, r...  71.1 us
    pallas_call x1, Pallas kernels, body(): pl.pallas_call(functools.partial(assemble, variables, rx), grid=(variable...  8.73 us

profile of v3, /device:TPU:0, one launch (start us, length us, event | category | flops | bytes accessed | tf_op | source)
XLA Modules:
  0.0 83.0 jit_solution(3170816860600688893)
XLA Ops:
  1.3 1.3 %sqrt_bitcast_fusion.gain = f32[4,64]{1,0:T(4,128)} fusion(f32[2,4,64]{2,1,0:T(4,128)} %rate_h.1), kind=kLoop, calls=%fused_computation | loop fusion | flops 768 | bytes 3072 | tf_op jit(solution)/shard_map/sqrt | solution.py:523
  2.6 71.1 %shard_map.122 = (f32[16,256,256]{2,1,0:T(8,128)}, f32[256,256]{1,0:T(8,128)}, f32[256,256]{1,0:T(8,128)}, f32[256,128]{1,0:T(8,128)}, f32[64,128]{1,0:T(8,128)}, /*index=5*/f32[1,512]{1,0:T(1,128)}) custom-call(f32[4,64]{1,0:T(4,128)} %sqrt_bitcast_fusion.gain, f32[4,1024,256]{2,1,0:T(8,128)} %bitcast.13, f32[4,1024,256]{2,1,0:T(8,128)} %bitcast.16, ...), custom_call_target="tpu_custom_call" | custom-call | tf_op jit(solution)/shard_map/pallas_call | solution.py:526
  73.7 0.0 copy-start
  73.7 8.7 %shard_map.123 = f32[4,1024,256]{2,1,0:T(8,128)} custom-call(f32[4,1024,256]{2,1,0:T(8,128)} %bitcast.14, f32[16,256,256]{2,1,0:T(8,128)} %get-tuple-element.8.field, f32[256,256]{1,0:T(8,128)} %get-tuple-element.9.row0, f32[256,256]{1,0:T(8,128)} %get-tuple-element.10.grow, f32[256,128]{1,0:T(8,128)} %get-tuple-element.11.axt, ...), custom_call_target="tpu_custom_call" | custom-call | tf_op jit(solution)/shard_map/pallas_call | solution.py:591
  82.5 0.0 copy-done
  82.5 0.6 copy.15
Async XLA Ops:
  73.7 8.7 %copy-start = (f32[1,512]{1,0:T(1,128)S(1)}, f32[1,512]{1,0:T(1,128)}, u32[]{:S(2)}) copy-start(f32[1,512]{1,0:T(1,128)} %get-tuple-element.13) | copy-start | bytes 6148

commit v4 on v2

--- a/solution.py
+++ b/solution.py
@@ -99,6 +99,14 @@
             source.at[v], target.at[v], send.at[v], recv.at[v], (other, gy), MESH
         )
 
+    pitch = rx + 1
+
+    def lay(slot, ref, v, tile, h):
+        for k in range(8):
+            stage[slot, k * pitch:k * pitch + rx, :] = ref[
+                v, pl.ds((tile * 8 + k) * rx, rx), half(h)
+            ]
+
     def half(h):
         return slice(h * LANES, (h + 1) * LANES)
 
@@ -113,7 +121,6 @@
         pl.semaphore_signal(barrier, inc=1, device_id=peer(offset), device_id_type=MESH)
     for copy in small:
         copy.wait()
-    pl.semaphore_wait(barrier, devices - 1)
 
     count = seen.shape[1]
     per = count // 2
@@ -129,7 +136,6 @@
             obs_all[me, 2 * number + part:2 * number + part + 1, :] = value[
                 :, part * per:(part + 1) * per
             ]
-    start_all(obs_all, obs_s, obs_r)
 
     raw[...] = jnp.zeros_like(raw)
     raw[:variables, :levels] = rate[0] * (1.0 / (rx * nx))
@@ -253,10 +259,10 @@
                 falls.append(fall)
                 decays.append(wide(ax))
                 for h in range(halves):
-                    stage[k * halves + h] = ctrl[v, pl.ds(tile * 8 * rx, 8 * rx), half(h)]
+                    lay(k * halves + h, ctrl, v, tile, h)
                 for x in range(rx):
                     strips = [
-                        stage[k * halves + h, pl.ds(x, 8, stride=rx), :] for h in range(halves)
+                        stage[k * halves + h, pl.ds(x, 8, stride=pitch), :] for h in range(halves)
                     ]
                     parts.append(jnp.concatenate(strips, axis=1) * up)
             parts = prefix(jnp.concatenate(parts, axis=0), tri)
@@ -274,6 +280,9 @@
                     field[x, rows, :] = state
                 edge[gy, pl.ds(tile * 8, 8), :] = column
 
+        if v == 0:
+            pl.semaphore_wait(barrier, devices - 1)
+            start_all(obs_all, obs_s, obs_r)
         if v == variables - 1:
             start_row(edge, e_s, e_r)
         step_forward(v)
@@ -284,13 +293,13 @@
     def _(tile):
         for v in range(variables):
             for h in range(halves):
-                stage[v * halves + h] = bg[v, pl.ds(tile * 8 * rx, 8 * rx), half(h)]
+                lay(v * halves + h, bg, v, tile, h)
         weights = [tab[2 * variables + v, pl.ds(tile * 8, 8), :] for v in range(variables)]
         for x in range(rx):
             for h in range(halves):
                 part = jnp.zeros((8, LANES), f32)
                 for v in range(variables):
-                    part = part + weights[v] * stage[v * halves + h, pl.ds(x, 8, stride=rx), :]
+                    part = part + weights[v] * stage[v * halves + h, pl.ds(x, 8, stride=pitch), :]
                 base_levels[x, pl.ds(tile * 8, 8), half(h)] = part
 
     step_forward(variables)
@@ -480,10 +489,11 @@
                 entering = ax * entering
                 value = field[x, mine, :] + reach * wide(q) + entering
                 for h in range(halves):
-                    stage[v * halves + h, pl.ds(x, 8, stride=rx), :] = value[:, half(h)]
+                    stage[v * halves + h, pl.ds(x, 8, stride=pitch), :] = value[:, half(h)]
             for h in range(halves):
-                at = (v, pl.ds(tile * 8 * rx, 8 * rx), half(h))
-                out[at] = ctrl[at] + stage[v * halves + h]
+                for k in range(8):
+                    at = (v, pl.ds((tile * 8 + k) * rx, rx), half(h))
+                    out[at] = ctrl[at] + stage[v * halves + h, k * pitch:k * pitch + rx, :]
 
     for v in range(variables):
         @pl.when(gx < nx - 1)
@@ -531,7 +541,7 @@
             pltpu.VMEM((variables, levels, ry), f32),
             pltpu.VMEM((vk, ry), f32),
             pltpu.VMEM((vk, LANES), f32),
-            pltpu.VMEM((variables * ry // LANES, 8 * rx, LANES), f32),
+            pltpu.VMEM((variables * ry // LANES, 8 * rx + 8, LANES), f32),
             pltpu.VMEM((rx, levels, ry), f32),
             pltpu.VMEM((2 * levels, vk), bf16),
             pltpu.VMEM((vk, 3 * levels), bf16),

time: 81.6 us -> 80.5 us (0.987)
  Pallas kernels: 73.6 us -> 72.5 us
    pallas_call x1, Pallas kernels: 73.6 us -> 72.5 us  [body(): pl.pallas_call(functools.partial(kernel, nx, ny, variables, levels, rx, r...]
where the time goes in v4:
time: 80.5 us; the launch traced here: 80.3 us
  Pallas kernels  72.5 us (90%)
  local copies, waits for them, and re-layouts  5.22 us (6%)
  other arithmetic  1.3 us (2%)
  between operations  1.29 us (2%)
    pallas_call x1, Pallas kernels, body(): pl.pallas_call(functools.partial(kernel, nx, ny, variables, levels, rx, r...  72.5 us
    unnamed x4, local copies, waits for them, and re-layouts  5.22 us

profile of v4, /device:TPU:0, one launch (start us, length us, event | category | flops | bytes accessed | tf_op | source)
XLA Modules:
  0.0 80.3 jit_solution(438142749008490438)
XLA Ops:
  1.3 1.3 %sqrt_bitcast_fusion.gain = f32[4,64]{1,0:T(4,128)} fusion(f32[2,4,64]{2,1,0:T(4,128)} %rate_h.1), kind=kLoop, calls=%fused_computation | loop fusion | flops 768 | bytes 3072 | tf_op jit(solution)/shard_map/sqrt | solution.py:519
  2.6 72.5 %shard_map.122 = (f32[4,1024,256]{2,1,0:T(8,128)}, f32[1,512]{1,0:T(1,128)}) custom-call(f32[4,64]{1,0:T(4,128)} %sqrt_bitcast_fusion.gain, f32[4,1024,256]{2,1,0:T(8,128)} %bitcast.13, f32[4,1024,256]{2,1,0:T(8,128)} %bitcast.14, f32[4,64,64]{2,1,0:T(8,128)} %vert_h.1, f32[2,4,64]{2,1,0:T(4,128)} %rate_h.1, f32[4,64]{1,0:T(4,128)} %flash_w_h.1, ...), custom_call_target="tpu_custom_call" | custom-call | tf_op jit(solution)/shard_map/pallas_call | solution.py:522
  75.1 0.0 copy-start
  75.1 4.6 %copy.16 = f32[4,64,16,256]{3,2,1,0:T(8,128)} copy(f32[4,64,16,256]{3,2,1,0:T(8,128)} %bitcast.15) | data formatting | bytes 8388608
  79.7 0.0 copy-done
  79.7 0.6 copy.17
Async XLA Ops:
  75.1 4.7 %copy-start = (f32[1,512]{1,0:T(1,128)S(1)}, f32[1,512]{1,0:T(1,128)}, u32[]{:S(2)}) copy-start(f32[1,512]{1,0:T(1,128)} %get-tuple-element.5) | copy-start | bytes 6148
